TPU v7x, 1024 devices: a whole 4x4x32 slice. The times are simulated.
1024 devices in a mesh: group: 32 (over x, y, core), member: 32 (over z).
Axes of the slice: x: 4, y: 4, z: 32, core: 2. Of those that a mesh axis runs over, the one named last changes fastest.
Arguments:
- rows: bfloat16 [262144, 1024], P(('group', 'member')), may hold values from -9 to 9
- top_ids: int32 [262144], P(('group', 'member')), may hold values from 0 to 4095, as said below
- border_ids: int32 [4096], P(('group', 'member')), may hold values from 0 to 4095, as said below
- centroids: bfloat16 [4096, 64, 1024], P(('group', 'member')), may hold values from -6 to 6
- mass: float32 [4096, 64], P(('group', 'member')), may hold values from 1 to 64
Outputs:
- refined: float32 [4096, 64, 1024], P(('group', 'member'))
- new_mass: float32 [4096, 64], P(('group', 'member'))
Inputs may be any that keep to these rules, and one draw needn't show every extreme that they name: `top_ids`: top cluster c lives on device c // 4 (devices numbered group-major, member index (c // 4) % 32). Every device holds exactly 8 rows whose top cluster lies on each member index. The rows held by the 32 devices of one group whose top cluster lies on one given device number at most 16; for every member index some device reaches that bound from every group, so it receives 512 rows. `border_ids`: the border cluster of a top cluster differs from it and lies on the same device or on the device with the next member index in the same group; on the device with the last member index it lies on the same device.
All inputs are finite; a program needn't handle non-finite values.
Results may differ from a plain program's by a relative error of at most 0.0037.
Values may be sent and summed in bfloat16 or wider, within the bound.
A program may use at most 32 MiB of HBM per device.

v0:
```python
import jax
import jax.numpy as jnp
from jax import lax
from jax.sharding import PartitionSpec as P

ITERS = 2


SOFTMAX_HEAT = 32.0
PRIOR = 4.0
BALANCE = 1.0
KEEP = 0.5


def for_sending(shard):

    def short(part):
        return part.astype(jnp.bfloat16) if part.dtype == jnp.float32 else part

    return jax.tree.map(short, shard)


def shifted(shard, axis, by):
    size = lax.axis_size(axis)
    pairs = [(i, i + by) for i in range(size) if 0 <= i + by < size]
    return lax.ppermute(shard, axis, pairs)


def rank_within(labels, classes):
    hits = (labels[:, None] == jnp.arange(classes, dtype=jnp.int32)[None, :]).astype(jnp.int32)
    before = jnp.cumsum(hits, axis=0) - hits
    return jnp.sum(before * hits, axis=1)


def body(rows, top_ids, border_ids, centroids, mass):
    members = lax.axis_size("member")
    groups = lax.axis_size("group")
    tok, width = rows.shape
    cluster_index, subcentroid_index = mass.shape
    per_member = tok // members
    dest_member = top_ids // cluster_index % members
    slot = dest_member * per_member + rank_within(dest_member, members)
    source = jnp.zeros((tok,), jnp.int32).at[slot].set(jnp.arange(tok, dtype=jnp.int32))
    send_rows = rows[source].reshape(members, per_member, width)
    send_ids = top_ids[source].reshape(members, per_member)
    pooled_rows, pooled_ids = (
        lax.all_to_all(send_rows, "member", split_axis=0, concat_axis=0, tiled=True),
        lax.all_to_all(send_ids, "member", split_axis=0, concat_axis=0, tiled=True),
    )
    pool_rows = pooled_rows.reshape(tok, width)
    pool_ids = pooled_ids.reshape(tok)
    dest_group = pool_ids // (cluster_index * members)
    capacity = 2 * tok // groups
    place = dest_group * capacity + rank_within(dest_group, groups)
    chosen = (
        jnp.full((groups * capacity,), tok, jnp.int32)
        .at[place]
        .set(jnp.arange(tok, dtype=jnp.int32))
    )
    padded_rows = jnp.concatenate([pool_rows, jnp.zeros((1, width), rows.dtype)], axis=0)
    padded_local = jnp.concatenate(
        [pool_ids % cluster_index, jnp.full((1,), -1, jnp.int32)], axis=0
    )
    out_rows = padded_rows[chosen].reshape(groups, capacity, width)
    out_local = padded_local[chosen].reshape(groups, capacity)
    got_rows, got_local = (
        lax.all_to_all(out_rows, "group", split_axis=0, concat_axis=0, tiled=True),
        lax.all_to_all(
            for_sending(out_local), "group", split_axis=0, concat_axis=0, tiled=True
        ).astype(out_local.dtype),
    )
    position_rows = got_rows.reshape(groups * capacity, width)
    slot_local = got_local.reshape(groups * capacity)
    member_count = position_rows.shape[0]
    base = (lax.axis_index("group") * members + lax.axis_index("member")) * cluster_index
    offsets = border_ids - base
    valid = slot_local >= 0
    blocks = jnp.arange(2 * cluster_index, dtype=jnp.int32)
    own_pick = slot_local[:, None] == blocks[None, :]
    border_of = jnp.sum(
        jnp.where(
            slot_local[:, None] == jnp.arange(cluster_index, dtype=jnp.int32)[None, :],
            offsets[None, :],
            0,
        ),
        axis=1,
    )
    border_pick = (border_of[:, None] == blocks[None, :]) & valid[:, None]
    state = centroids.astype(jnp.float32)
    mass_now = mass
    scoring = centroids
    half = cluster_index * subcentroid_index
    for step in range(ITERS):
        bias = (BALANCE * jnp.log(mass_now)).astype(jnp.bfloat16)
        next_cent, next_bias = shifted((scoring, bias), "member", -1)
        cands = jnp.concatenate([scoring, next_cent], axis=0).reshape(2 * half, width)
        contender_bias = (
            jnp.concatenate([bias, next_bias], axis=0).reshape(2 * half).astype(jnp.float32)
        )
        contender_squared_norm = jnp.sum(jnp.square(cands.astype(jnp.float32)), axis=1)
        inner_products = lax.dot_general(
            position_rows, cands, (((1,), (1,)), ((), ())), preferred_element_type=jnp.float32
        )
        logit_matrix = (
            (2.0 * inner_products - contender_squared_norm) / SOFTMAX_HEAT - contender_bias
        ).reshape(member_count, 2 * cluster_index, subcentroid_index)
        own_sel = jnp.sum(jnp.where(own_pick[:, :, None], logit_matrix, 0.0), axis=1)
        border_sel = jnp.sum(jnp.where(border_pick[:, :, None], logit_matrix, 0.0), axis=1)
        joined = jnp.concatenate([own_sel, border_sel], axis=1)
        top = jnp.max(joined, axis=1, keepdims=True)
        expo = jnp.exp(joined - top)
        weight = jnp.where(valid[:, None], expo / jnp.sum(expo, axis=1, keepdims=True), 0.0).astype(
            jnp.bfloat16
        )
        spread = jnp.where(
            own_pick[:, :, None], weight[:, None, :subcentroid_index], 0
        ) + jnp.where(border_pick[:, :, None], weight[:, None, subcentroid_index:], 0)
        spread_flat = spread.reshape(member_count, 2 * half)
        totals = lax.dot_general(
            spread_flat, position_rows, (((0,), (0,)), ((), ())), preferred_element_type=jnp.float32
        )
        counts = jnp.sum(spread_flat.astype(jnp.float32), axis=0)
        own_totals = totals[:half]
        own_counts = counts[:half]
        came, came_counts = shifted((totals[half:], counts[half:]), "member", 1)
        sums = (own_totals + came).reshape(cluster_index, subcentroid_index, width)
        count_all = (own_counts + came_counts).reshape(cluster_index, subcentroid_index)
        state = (PRIOR * state + sums) / (PRIOR + count_all)[:, :, None]
        mass_now = KEEP * mass_now + count_all
        scoring = state.astype(jnp.bfloat16)
    return (state, mass_now)


def solution(mesh):
    in_specs = (
        P(("group", "member"), None),
        P(("group", "member")),
        P(("group", "member")),
        P(("group", "member"), None, None),
        P(("group", "member"), None),
    )
    out_specs = (P(("group", "member"), None, None), P(("group", "member"), None))
    return jax.shard_map(body, mesh=mesh, in_specs=in_specs, out_specs=out_specs, check_vma=False)
```

profile of v0, /device:TPU:32, one launch (start us, length us, event | category | flops | bytes accessed | tf_op | source)
XLA Modules:
  0.0 247.5 jit_solution(16596200312502799629)
XLA Ops:
  0.6 0.8 fusion.39
  1.4 0.7 and_select_fusion.4
  2.1 0.6 reduce-window.14
  2.7 0.2 slice_reduce_fusion.1
  2.9 0.1 fusion.16
  3.0 0.7 compare_select_fusion.3
  3.7 1.4 scatter_custom_fusion
  5.2 2.0 gather_fusion
  7.2 0.7 all_to_all.18
  7.8 28.6 %all-to-all-start = ((s32[32,1,8]{2,1,0:T(1,128)}), s32[32,1,8]{2,1,0:T(1,128)S(1)}, u32[]{:S(2)}, u32[]{:S(2)}) async-start(s32[32,1,8]{2,1,0:T(1,128)} %bitcast.2), calls=%async_computation | async-start | bytes 32768 | tf_op jit(solution)/shard_map/all_to_all | solution.py:48
  36.5 2.0 gather_fusion.2
  38.5 18.7 %all-to-all-done = s32[32,1,8]{2,1,0:T(1,128)S(1)} async-done(((s32[32,1,8]{2,1,0:T(1,128)}), s32[32,1,8]{2,1,0:T(1,128)S(1)}, u32[]{:S(2)}, u32[]{:S(2)}) %all-to-all-start) | async-done | bytes 1056 | tf_op jit(solution)/shard_map/all_to_all | solution.py:48
  57.2 5.3 %all-to-all-start.2 = ((bf16[32,8,1024]{2,1,0:T(8,128)(2,1)}), bf16[32,8,1024]{2,1,0:T(8,128)(2,1)S(1)}, u32[]{:S(2)}, u32[]{:S(2)}) async-start(bf16[32,8,1024]{2,1,0:T(8,128)(2,1)} %bitcast.7), calls=%async_computation.2 | async-start | bytes 1048576 | tf_op jit(solution)/shard_map/all_to_all | solution.py:47
  62.5 2.3 collective-permute-start.1
  64.8 1.9 collective-permute-start
  66.7 0.1 reshape.359
  66.8 0.1 reshape.360
  66.9 0.5 broadcast.367
  67.4 0.7 reduce.22
  68.1 0.1 reshape.358
  68.2 0.6 reduce-window.16
  68.8 0.2 slice_reduce_fusion
  69.1 0.1 fusion.13
  69.2 1.4 scatter_custom_fusion.1
  70.6 3.5 %gather_fusion.1 = s32[512]{0:T(512)S(1)} fusion(s32[257]{0:T(512)S(1)} %pad_add_fusion, s32[1024]{0:T(1024)S(1)} %pad_clamp_fusion), kind=kCustom, calls=%fused_computation.1 | custom fusion | bytes 6144 | tf_op jit(solution)/shard_map/gather | solution.py:65
  74.1 0.7 all_to_all.20
  74.8 51.5 %all-to-all-done.2 = bf16[32,8,1024]{2,1,0:T(8,128)(2,1)S(1)} async-done(((bf16[32,8,1024]{2,1,0:T(8,128)(2,1)}), bf16[32,8,1024]{2,1,0:T(8,128)(2,1)S(1)}, u32[]{:S(2)}, u32[]{:S(2)}) %all-to-all-start.2) | async-done | bytes 524320 | tf_op jit(solution)/shard_map/all_to_all | solution.py:47
  126.3 7.3 %all-to-all-start.1 = ((s32[32,1,16]{2,1,0:T(1,128)}), s32[32,1,16]{2,1,0:T(1,128)S(1)}, u32[]{:S(2)}, u32[]{:S(2)}) async-start(s32[32,1,16]{2,1,0:T(1,128)} %bitcast.6), calls=%async_computation.1 | async-start | bytes 32768 | tf_op jit(solution)/shard_map/all_to_all | solution.py:68
  133.7 2.8 %gather_fusion.3 = bf16[512,1024]{1,0:T(8,128)(2,1)} fusion(bf16[257,1024]{1,0:T(8,128)(2,1)S(1)} %concatenate.25, s32[1024]{0:T(1024)S(1)} %pad_clamp_fusion), kind=kCustom, calls=%fused_computation.3 | custom fusion | bytes 2099200 | tf_op jit(solution)/shard_map/gather | solution.py:64
  136.5 4.5 %all-to-all-done.1 = s32[32,1,16]{2,1,0:T(1,128)S(1)} async-done(((s32[32,1,16]{2,1,0:T(1,128)}), s32[32,1,16]{2,1,0:T(1,128)S(1)}, u32[]{:S(2)}, u32[]{:S(2)}) %all-to-all-start.1) | async-done | bytes 2080 | tf_op jit(solution)/shard_map/all_to_all | solution.py:68
  141.0 3.9 %all-to-all-start.3 = ((bf16[32,16,1024]{2,1,0:T(8,128)(2,1)}), bf16[32,16,1024]{2,1,0:T(8,128)(2,1)S(1)}, u32[]{:S(2)}, u32[]{:S(2)}) async-start(bf16[32,16,1024]{2,1,0:T(8,128)(2,1)} %bitcast.9), calls=%async_computation.3 | async-start | bytes 2097152 | tf_op jit(solution)/shard_map/all_to_all | solution.py:67
  145.1 0.7 reduce.23
  145.9 0.1 select_reduce_fusion.4
  146.0 1.1 constant_dynamic-update-slice_fusion
  147.1 0.3 multiply_reduce_fusion.1
  147.5 14.3 %all-to-all-done.3 = bf16[32,16,1024]{2,1,0:T(8,128)(2,1)S(1)} async-done(((bf16[32,16,1024]{2,1,0:T(8,128)(2,1)}), bf16[32,16,1024]{2,1,0:T(8,128)(2,1)S(1)}, u32[]{:S(2)}, u32[]{:S(2)}) %all-to-all-start.3) | async-done | bytes 1048608 | tf_op jit(solution)/shard_map/all_to_all | solution.py:67
  161.8 0.7 fusion.3
  162.5 0.2 select_reduce_fusion.3
  162.9 0.1 select_add_fusion.1
  163.0 0.7 fusion.29
  163.7 1.3 copy-done.2
  165.1 1.9 collective-permute-start.2
  167.1 0.3 convert_reduce_fusion.1
  167.4 3.1 %collective-permute-start.3 = (f32[256]{0:T(256)S(1)}, f32[256]{0:T(256)S(1)}, u32[]{:S(2)}, u32[]{:S(2)}) collective-permute-start(f32[256]{0:T(256)S(1)} %slice.71), channel_id=1, source_target_pairs={{0,1},{1,2},{2,3},{3,4},{4,5},{5,6},{6,7},{7,8},{8,9},{9,10},{10,1... | collective-permute-start | bytes 3080 | tf_op jit(solution)/shard_map/ppermute | solution.py:26
  170.6 22.0 %collective-permute-done.3 = f32[256]{0:T(256)S(1)} collective-permute-done((f32[256]{0:T(256)S(1)}, f32[256]{0:T(256)S(1)}, u32[]{:S(2)}, u32[]{:S(2)}) %collective-permute-start.3) | collective-permute-done | bytes 1056 | tf_op jit(solution)/shard_map/ppermute | solution.py:26
  192.7 1.7 slice_add_fusion.1
  194.4 1.0 fusion.10
  195.4 1.9 collective-permute-start.4
  197.3 2.1 collective-permute-start.5
  199.4 11.6 %collective-permute-done.5 = bf16[4,64]{1,0:T(4,128)(2,1)S(1)} collective-permute-done((bf16[4,64]{1,0:T(4,128)(2,1)S(1)}, bf16[4,64]{1,0:T(4,128)(2,1)S(1)}, u32[]{:S(2)}, u32[]{:S(2)}) %collective-permute-start.5) | collective-permute-done | bytes 544 | tf_op jit(solution)/shard_map/ppermute | solution.py:26
  211.0 1.5 multiply_reduce_fusion
  212.6 1.3 pad_maximum_fusion
  213.9 0.7 fusion.5
  214.6 0.2 select_reduce_fusion.1
  215.1 0.7 fusion.30
  215.8 1.3 copy-done.1
  217.2 1.1 slice.97
  218.3 2.4 collective-permute-start.6
  220.7 0.3 convert_reduce_fusion
  221.1 3.7 %collective-permute-start.7 = (f32[256]{0:T(256)S(1)}, f32[256]{0:T(256)S(1)}, u32[]{:S(2)}, u32[]{:S(2)}) collective-permute-start(f32[256]{0:T(256)S(1)} %slice.79), channel_id=1, source_target_pairs={{0,1},{1,2},{2,3},{3,4},{4,5},{5,6},{6,7},{7,8},{8,9},{9,10},{10,1... | collective-permute-start | bytes 3080 | tf_op jit(solution)/shard_map/ppermute | solution.py:26
  224.9 19.2 %collective-permute-done.7 = f32[256]{0:T(256)S(1)} collective-permute-done((f32[256]{0:T(256)S(1)}, f32[256]{0:T(256)S(1)}, u32[]{:S(2)}, u32[]{:S(2)}) %collective-permute-start.7) | collective-permute-done | bytes 1056 | tf_op jit(solution)/shard_map/ppermute | solution.py:26
  244.2 0.6 multiply_add_fusion
  244.8 1.4 slice_add_fusion
  246.2 1.3 add_divide_fusion
  (69 shorter events, 1.8 us)
Async XLA Ops:
  0.6 35.8 %copy-start = (bf16[256,1024]{1,0:T(8,128)(2,1)S(1)}, bf16[256,1024]{1,0:T(8,128)(2,1)}, u32[]{:S(2)}) copy-start(bf16[256,1024]{1,0:T(8,128)(2,1)} %param.5) | copy-start | bytes 1572868
  7.8 49.3 %all-to-all-start = ((s32[32,1,8]{2,1,0:T(1,128)}), s32[32,1,8]{2,1,0:T(1,128)S(1)}, u32[]{:S(2)}, u32[]{:S(2)}) async-start(s32[32,1,8]{2,1,0:T(1,128)} %bitcast.2), calls=%async_computation | async-start | bytes 32768 | tf_op jit(solution)/shard_map/all_to_all | solution.py:48
  36.5 26.0 %copy-start.4 = (f32[4,64]{1,0:T(4,128)S(1)}, f32[4,64]{1,0:T(4,128)}, u32[]{:S(2)}) copy-start(f32[4,64]{1,0:T(4,128)} %param.9) | copy-start | bytes 3076
  36.5 28.3 %copy-start.3 = (bf16[4,64,1024]{2,1,0:T(8,128)(2,1)S(1)}, bf16[4,64,1024]{2,1,0:T(8,128)(2,1)}, u32[]{:S(2)}) copy-start(bf16[4,64,1024]{2,1,0:T(8,128)(2,1)} %param.8) | copy-start | bytes 1572868
  38.5 95.2 %copy-start.5 = (s32[4]{0:T(128)S(1)}, s32[4]{0:T(128)}, u32[]{:S(2)}) copy-start(s32[4]{0:T(128)} %param.7) | copy-start | bytes 52
  57.2 69.2 %all-to-all-start.2 = ((bf16[32,8,1024]{2,1,0:T(8,128)(2,1)}), bf16[32,8,1024]{2,1,0:T(8,128)(2,1)S(1)}, u32[]{:S(2)}, u32[]{:S(2)}) async-start(bf16[32,8,1024]{2,1,0:T(8,128)(2,1)} %bitcast.7), calls=%async_computation.2 | async-start | bytes 1048576 | tf_op jit(solution)/shard_map/all_to_all | solution.py:47
  62.5 82.5 %collective-permute-start.1 = (bf16[4,64]{1,0:T(4,128)(2,1)S(1)}, bf16[4,64]{1,0:T(4,128)(2,1)S(1)}, u32[]{:S(2)}, u32[]{:S(2)}) collective-permute-start(bf16[4,64]{1,0:T(4,128)(2,1)S(1)} %log_convert_fusion.1), channel_id=1, source_target_pairs={{1,0},{2,1},{3,2},{4,3},{5,4},{6,5},{7,6},{8,7},{9,8},{10,9},{11,1... | collective-permute-start | bytes 1544 | tf_op jit(solution)/shard_map/ppermute | solution.py:26
  64.8 81.2 %collective-permute-start = (bf16[4,64,1024]{2,1,0:T(8,128)(2,1)S(1)}, bf16[4,64,1024]{2,1,0:T(8,128)(2,1)}, u32[]{:S(2)}, u32[]{:S(2)}) collective-permute-start(bf16[4,64,1024]{2,1,0:T(8,128)(2,1)S(1)} %copy-done.3), channel_id=1, source_target_pairs={{1,0},{2,1},{3,2},{4,3},{5,4},{6,5},{7,6},{8,7},{9,8},{10,9},{11,1... | collective-permute-start | bytes 1572872 | tf_op jit(solution)/shard_map/ppermute | solution.py:26
  126.3 14.7 %all-to-all-start.1 = ((s32[32,1,16]{2,1,0:T(1,128)}), s32[32,1,16]{2,1,0:T(1,128)S(1)}, u32[]{:S(2)}, u32[]{:S(2)}) async-start(s32[32,1,16]{2,1,0:T(1,128)} %bitcast.6), calls=%async_computation.1 | async-start | bytes 32768 | tf_op jit(solution)/shard_map/all_to_all | solution.py:68
  141.0 20.7 %all-to-all-start.3 = ((bf16[32,16,1024]{2,1,0:T(8,128)(2,1)}), bf16[32,16,1024]{2,1,0:T(8,128)(2,1)S(1)}, u32[]{:S(2)}, u32[]{:S(2)}) async-start(bf16[32,16,1024]{2,1,0:T(8,128)(2,1)} %bitcast.9), calls=%async_computation.3 | async-start | bytes 2097152 | tf_op jit(solution)/shard_map/all_to_all | solution.py:67
  163.7 1.4 copy-start.2
  165.1 27.5 %collective-permute-start.2 = (f32[256,1024]{1,0:T(8,128)S(1)}, f32[256,1024]{1,0:T(8,128)}, u32[]{:S(2)}, u32[]{:S(2)}) collective-permute-start(f32[256,1024]{1,0:T(8,128)S(1)} %slice.93), channel_id=1, source_target_pairs={{0,1},{1,2},{2,3},{3,4},{4,5},{5,6},{6,7},{7,8},{8,9},{9,10},{10,1... | collective-permute-start | bytes 3145736 | tf_op jit(solution)/shard_map/ppermute | solution.py:26
  167.4 25.1 %collective-permute-start.3 = (f32[256]{0:T(256)S(1)}, f32[256]{0:T(256)S(1)}, u32[]{:S(2)}, u32[]{:S(2)}) collective-permute-start(f32[256]{0:T(256)S(1)} %slice.71), channel_id=1, source_target_pairs={{0,1},{1,2},{2,3},{3,4},{4,5},{5,6},{6,7},{7,8},{8,9},{9,10},{10,1... | collective-permute-start | bytes 3080 | tf_op jit(solution)/shard_map/ppermute | solution.py:26
  195.4 15.7 %collective-permute-start.4 = (bf16[4,64,1024]{2,1,0:T(8,128)(2,1)}, bf16[4,64,1024]{2,1,0:T(8,128)(2,1)}, u32[]{:S(2)}, u32[]{:S(2)}) collective-permute-start(bf16[4,64,1024]{2,1,0:T(8,128)(2,1)} %fusion.10), channel_id=1, source_target_pairs={{1,0},{2,1},{3,2},{4,3},{5,4},{6,5},{7,6},{8,7},{9,8},{10,9},{11,1... | collective-permute-start | bytes 1572872 | tf_op jit(solution)/shard_map/ppermute | solution.py:26
  197.3 13.7 %collective-permute-start.5 = (bf16[4,64]{1,0:T(4,128)(2,1)S(1)}, bf16[4,64]{1,0:T(4,128)(2,1)S(1)}, u32[]{:S(2)}, u32[]{:S(2)}) collective-permute-start(bf16[4,64]{1,0:T(4,128)(2,1)S(1)} %get-tuple-element.16), channel_id=1, source_target_pairs={{1,0},{2,1},{3,2},{4,3},{5,4},{6,5},{7,6},{8,7},{9,8},{10,9},{11,1... | collective-permute-start | bytes 1544 | tf_op jit(solution)/shard_map/ppermute | solution.py:26
  215.8 1.4 copy-start.1
  218.3 26.5 %collective-permute-start.6 = (f32[256,1024]{1,0:T(8,128)}, f32[256,1024]{1,0:T(8,128)S(1)}, u32[]{:S(2)}, u32[]{:S(2)}) collective-permute-start(f32[256,1024]{1,0:T(8,128)} %slice.97), channel_id=1, source_target_pairs={{0,1},{1,2},{2,3},{3,4},{4,5},{5,6},{6,7},{7,8},{8,9},{9,10},{10,1... | collective-permute-start | bytes 3145736 | tf_op jit(solution)/shard_map/ppermute | solution.py:26
  221.1 23.1 %collective-permute-start.7 = (f32[256]{0:T(256)S(1)}, f32[256]{0:T(256)S(1)}, u32[]{:S(2)}, u32[]{:S(2)}) collective-permute-start(f32[256]{0:T(256)S(1)} %slice.79), channel_id=1, source_target_pairs={{0,1},{1,2},{2,3},{3,4},{4,5},{5,6},{6,7},{7,8},{8,9},{9,10},{10,1... | collective-permute-start | bytes 3080 | tf_op jit(solution)/shard_map/ppermute | solution.py:26
where the time goes:
time: 248 us; the launch traced here: 247 us
  waiting for transfers between devices  142 us (57%)
  starting transfers between devices  64.5 us (26%)
  local copies, waits for them, and re-layouts  21.5 us (9%)
  other arithmetic  15.6 us (6%)
  matrix products  2.91 us (1%)
    ppermute x8, waiting for transfers between devices, shifted(): return lax.ppermute(shard, axis, pairs)  52.8 us
    all_to_all x1, waiting for transfers between devices, body(): lax.all_to_all(send_rows, 'member', split_axis=0, concat_axis=0, tiled=True)  51.5 us
    all_to_all x1, starting transfers between devices, body(): lax.all_to_all(send_ids, 'member', split_axis=0, concat_axis=0, tiled=True)  28.6 us
    ppermute x8, starting transfers between devices, shifted(): return lax.ppermute(shard, axis, pairs)  19.3 us
    all_to_all x1, waiting for transfers between devices, body(): lax.all_to_all(send_ids, 'member', split_axis=0, concat_axis=0, tiled=True)  18.7 us
    all_to_all x1, waiting for transfers between devices, body(): lax.all_to_all(out_rows, 'group', split_axis=0, concat_axis=0, tiled=True)  14.3 us
    all_to_all x1, starting transfers between devices, body(): lax.all_to_all(for_sending(out_local), 'group', split_axis=0, concat_axis...  7.32 us
    all_to_all x1, starting transfers between devices, body(): lax.all_to_all(send_rows, 'member', split_axis=0, concat_axis=0, tiled=True)  5.32 us
  transfers between devices with their start and end apart: 12, of which 7 were waited for; matrix products, arithmetic and copies ran while one was open for 7% of the time, Pallas kernels for 0%

commit v1 on v0

v1 whole, which is shorter than its diff:
```python
import functools

import jax
import jax.numpy as jnp
from jax import lax
from jax.experimental import pallas as pl
from jax.experimental.pallas import tpu as pltpu
from jax.sharding import PartitionSpec as P

ITERS = 2
SOFTMAX_HEAT = 32.0
PRIOR = 4.0
BALANCE = 1.0
KEEP = 0.5

CHUNKS = 2
LANES = 128
LOW = -1e30
MESH = pl.DeviceIdType.MESH
F32, BF16, I32 = jnp.float32, jnp.bfloat16, jnp.int32


def log2(n):
    assert n & (n - 1) == 0
    return n.bit_length() - 1


def iota(shape, dim):
    return lax.broadcasted_iota(I32, shape, dim)


def onehot(cond):
    return jnp.where(cond, 1.0, 0.0).astype(BF16)


def dot(a, b):
    return jnp.dot(a, b, preferred_element_type=F32)


def dot_t(a, b):
    return lax.dot_general(a, b, (((1,), (1,)), ((), ())), preferred_element_type=F32)


def lane_row(row, matrix):
    many = jnp.broadcast_to(row.astype(F32), (16, row.shape[1])).astype(BF16)
    return dot_t(many, matrix)[0:1].astype(I32)


def ranked(label, classes):
    n = label.shape[1]
    hit = iota((classes, n), 0) == label
    before = dot(onehot(hit), onehot(iota((n, n), 0) < iota((n, n), 1)))
    return jnp.sum(jnp.where(hit, before, 0.0), axis=0, keepdims=True).astype(I32)


def kernel(
    M, G,
    rows_ref, ids_ref, border_ref, cent_ref, mass_ref,
    out_ref, mass_out_ref,
    rsend, ra, rb, gsx, gsy, x, y,
    idmsg, ida, idb, locmsg, locx, ymsg, yrecv, st_send, st_recv,
    ids_s, ids_r, idf_s, idf_r, row_s, row_r, fwd_s, fwd_r,
    loc_s, loc_r, grp_s, grp_r, y_s, y_r, st_s, st_r,
):
    tok, D = rows_ref.shape
    C, SUB = mass_ref.shape
    K = C * SUB
    pm = tok // M
    slab = 2 * pm
    half = M // 2
    cap = 2 * tok // G
    slots = G * cap
    W = D // CHUNKS
    H = W // 2
    g = lax.axis_index("group")
    m = lax.axis_index("member")
    right = {"member": (m + 1) % M}
    left = {"member": (m + M - 1) % M}

    def remote(src, dst, ssem, rsem, dev):
        return pltpu.make_async_remote_copy(
            src_ref=src, dst_ref=dst, send_sem=ssem, recv_sem=rsem,
            device_id=dev, device_id_type=MESH)

    def wait(ref, sem):
        pltpu.make_async_copy(ref, ref, sem).wait()

    barrier = pltpu.get_barrier_semaphore()

    @pl.loop(1, M)
    def _(d):
        pl.semaphore_signal(barrier, inc=1, device_id={"member": (m + d) % M}, device_id_type=MESH)

    @pl.loop(1, G)
    def _(j):
        pl.semaphore_signal(barrier, inc=1, device_id={"group": (g + j) % G}, device_id_type=MESH)

    ids = ids_ref[...]
    rel = (((ids >> log2(C)) & (M - 1)) - m) & (M - 1)
    slot = rel * pm + ranked(rel, M)
    coded = ((ids >> log2(C * M)) << log2(C)) | (ids & (C - 1))
    ordered = lane_row(coded, onehot(iota((tok, tok), 0) == slot))
    per = LANES // pm
    for b in range(tok // LANES):
        part = ordered[:, b * LANES:(b + 1) * LANES].reshape(1, 1, LANES)
        keep = iota((per, 1, LANES), 2) >> log2(pm) == iota((per, 1, LANES), 0)
        idmsg[b * per:(b + 1) * per] = jnp.where(keep, part, 0)
    q = iota((2 * tok, tok), 0)
    same = ((q >> log2(slab)) * pm + (q & (pm - 1))) == slot
    second = ((q >> log2(pm)) & 1) == 1
    pick0 = onehot(same & ~second)
    pick1 = onehot(same & second)

    def order_rows(c):
        rsend[c] = (dot(pick0, rows_ref[:, c * W:c * W + H])
                    + dot(pick1, rows_ref[:, c * W + H:(c + 1) * W])).astype(BF16)

    order_rows(0)
    pl.semaphore_wait(barrier, M - 1 + G - 1)

    @pl.loop(1, half)
    def _(d):
        remote(idmsg.at[d], ida.at[d], ids_s.at[0], ids_r.at[0], {"member": (m + d) % M}).start()
        e = M - 1 - d
        remote(idmsg.at[e], idb.at[e], ids_s.at[1], ids_r.at[1], {"member": (m + M - d) % M}).start()

    ida[0] = idmsg[0]
    idb[M - 1] = idmsg[M - 1]

    def at(d):
        return pl.ds(pl.multiple_of(d * slab, slab), slab)

    def send_rows(c):
        @pl.loop(1, half)
        def _(d):
            e = M - 1 - d
            remote(rsend.at[c, at(d)], ra.at[c, at(d)], row_s.at[c, 0], row_r.at[c, 0],
                   {"member": (m + d) % M}).start()
            remote(rsend.at[c, at(e)], rb.at[c, at(e)], row_s.at[c, 1], row_r.at[c, 1],
                   {"member": (m + M - d) % M}).start()
        ra[c, 0:slab] = rsend[c, 0:slab]
        rb[c, (M - 1) * slab:] = rsend[c, (M - 1) * slab:]

    send_rows(0)
    for c in range(1, CHUNKS):
        order_rows(c)
        send_rows(c)

    wait(ida.at[1:half], ids_r.at[0])
    remote(ida.at[0:half], idb.at[0:half], idf_s.at[0], idf_r.at[0], right).start()
    wait(idb.at[half:M - 1], ids_r.at[1])
    remote(idb.at[half:M], ida.at[half:M], idf_s.at[1], idf_r.at[1], left).start()
    wait(ida.at[half:M], idf_r.at[1])
    wait(idb.at[0:half], idf_r.at[0])

    def group_place(ref):
        code = jnp.concatenate(
            [jnp.sum(ref[b * per:(b + 1) * per], axis=0) for b in range(tok // LANES)], axis=1)
        toward = ((code >> log2(C)) - g) & (G - 1)
        rank = ranked(toward, G)
        return code, toward, rank

    def group_picks(toward, rank):
        wide = iota((2 * tok, tok), 0)
        spread = onehot(((wide >> log2(slab)) * pm + (wide & (pm - 1))) == iota((2 * tok, tok), 1))
        place = lane_row(toward, spread) * cap + lane_row(rank, spread)
        fits = iota((slots, 2 * tok), 0) == place
        upper = ((iota((slots, 2 * tok), 1) >> log2(pm)) & 1) == 1
        return onehot(fits & ~upper), onehot(fits & upper)

    code, toward, rank = group_place(ida)
    local1 = lane_row((code & (C - 1)) + 1, onehot(iota((slots, tok), 0) == toward * cap + rank))
    pj = max(LANES // cap, 1)
    span = max(LANES, cap)
    for b in range(slots // span):
        part = local1[:, b * span:(b + 1) * span].reshape(1, 1, span)
        keep = iota((pj, 1, span), 2) >> log2(cap) == iota((pj, 1, span), 0)
        locmsg[b * pj:(b + 1) * pj] = jnp.where(keep, part, 0)

    @pl.loop(1, G)
    def _(j):
        remote(locmsg.at[j], locx.at[j], loc_s, loc_r, {"group": (g + j) % G}).start()

    locx[0] = locmsg[0]
    xp = group_picks(toward, rank)
    _, toward_b, rank_b = group_place(idb)
    yp = group_picks(toward_b, rank_b)

    wait(locx.at[1:G], loc_r)
    local = jnp.concatenate(
        [jnp.sum(locx[b * pj:(b + 1) * pj], axis=0) for b in range(slots // span)], axis=1) - 1
    base = (g * M + m) * C
    edge = jnp.full((1, slots), -1, I32)
    for k in range(C):
        edge = jnp.where(local == k, border_ref[:, k:k + 1] - base, edge)
    ymsg[...] = jnp.where(local >= 0, edge - C, -1)
    remote(ymsg, yrecv, y_s, y_r, right).start()

    def gat(j):
        return pl.ds(pl.multiple_of(j * cap, cap), cap)

    def forward(c):
        wait(ra.at[c, slab:half * slab], row_r.at[c, 0])
        remote(ra.at[c, 0:half * slab], rb.at[c, 0:half * slab],
               fwd_s.at[c, 0], fwd_r.at[c, 0], right).start()
        wait(rb.at[c, half * slab:(M - 1) * slab], row_r.at[c, 1])
        remote(rb.at[c, half * slab:], ra.at[c, half * slab:],
               fwd_s.at[c, 1], fwd_r.at[c, 1], left).start()

    def regroup(c, which):
        pool, send, land, picks = ((ra, gsx, x, xp), (rb, gsy, y, yp))[which]
        if which == 0:
            wait(ra.at[c, half * slab:], fwd_r.at[c, 1])
        else:
            wait(rb.at[c, 0:half * slab], fwd_r.at[c, 0])
        have = pool[c]
        for h in range(2):
            send[c, :, h * H:(h + 1) * H] = dot(picks[h], have).astype(BF16)

        @pl.loop(1, G)
        def _(j):
            remote(send.at[c, gat(j)], land.at[c, gat(j)], grp_s.at[c, which], grp_r.at[c, which],
                   {"group": (g + j) % G}).start()
        land[c, 0:cap] = send[c, 0:cap]

    for c in range(CHUNKS):
        forward(c)
        regroup(c, 0)
        regroup(c, 1)

    eye = iota((SUB, SUB), 0) == iota((SUB, SUB), 1)

    def to_column(table):
        return jnp.concatenate(
            [jnp.sum(jnp.where(eye, table[k:k + 1], 0.0), axis=1, keepdims=True)
             for k in range(C)], axis=0)

    block = iota((K, 1), 0) >> log2(SUB)
    wait(yrecv, y_r)
    mask_x = (block == local) | (block == edge)
    mask_y = block == yrecv[...]
    mass_now = to_column(mass_ref[...])
    for step in range(ITERS):
        bias = (BALANCE * jnp.log(mass_now)).astype(BF16).astype(F32)
        if step == 0:
            scoring = cent_ref
            state = cent_ref[...].astype(F32)
        else:
            scoring = out_ref[...].astype(BF16)
            state = out_ref[...]
        norm = jnp.sum(jnp.square(scoring[...].astype(F32)), axis=1, keepdims=True)
        lx = jnp.zeros((K, slots), F32)
        ly = jnp.zeros((K, slots), F32)
        for c in range(CHUNKS):
            part = scoring[:, c * W:(c + 1) * W]
            if step == 0:
                wait(x.at[c, cap:], grp_r.at[c, 0])
            lx = lx + dot_t(part, x[c])
            if step == 0:
                wait(y.at[c, cap:], grp_r.at[c, 1])
            ly = ly + dot_t(part, y[c])

        def local_terms(product, mask, slot_at):
            logit = jnp.where(mask, (2.0 * product - norm) / SOFTMAX_HEAT - bias, LOW)
            top = jnp.max(logit, axis=0, keepdims=True)
            expo = jnp.where(mask, jnp.exp(logit - top), 0.0)
            total = jnp.sum(expo, axis=0, keepdims=True)
            st_send[slot_at, :, 0:slots] = top
            st_send[slot_at, :, slots:] = total
            return expo, top, total

        ix, iy = 2 * step, 2 * step + 1
        ex, tx, sx = local_terms(lx, mask_x, ix)
        remote(st_send.at[ix], st_recv.at[ix], st_s.at[ix], st_r.at[ix], right).start()
        ey, ty, sy = local_terms(ly, mask_y, iy)
        remote(st_send.at[iy], st_recv.at[iy], st_s.at[iy], st_r.at[iy], left).start()

        def weights(expo, top, total, slot_at):
            wait(st_recv.at[slot_at], st_r.at[slot_at])
            other_top = st_recv[slot_at, :, 0:slots]
            other_total = st_recv[slot_at, :, slots:]
            most = jnp.maximum(top, other_top)
            mine = jnp.exp(top - most)
            whole = total * mine + other_total * jnp.exp(other_top - most)
            return (expo * (mine / jnp.where(whole > 0.0, whole, 1.0))).astype(BF16)

        wx = weights(ex, tx, sx, iy)
        wy = weights(ey, ty, sy, ix)
        count = (jnp.sum(wx.astype(F32), axis=1, keepdims=True)
                 + jnp.sum(wy.astype(F32), axis=1, keepdims=True))
        scale = 1.0 / (PRIOR + count)
        for c in range(CHUNKS):
            cols = slice(c * W, (c + 1) * W)
            sums = dot(wx, x[c]) + dot(wy, y[c])
            out_ref[:, cols] = (PRIOR * state[:, cols] + sums) * scale
        mass_now = KEEP * mass_now + count
    for k in range(C):
        mass_out_ref[k:k + 1, :] = jnp.sum(
            jnp.where(eye, mass_now[k * SUB:(k + 1) * SUB], 0.0), axis=0, keepdims=True)

    wait(idmsg.at[1:half], ids_s.at[0])
    wait(idmsg.at[half:M - 1], ids_s.at[1])
    wait(ida.at[0:half], idf_s.at[0])
    wait(idb.at[half:M], idf_s.at[1])
    wait(locmsg.at[1:G], loc_s)
    wait(ymsg, y_s)
    for c in range(CHUNKS):
        wait(rsend.at[c, slab:half * slab], row_s.at[c, 0])
        wait(rsend.at[c, half * slab:(M - 1) * slab], row_s.at[c, 1])
        wait(ra.at[c, 0:half * slab], fwd_s.at[c, 0])
        wait(rb.at[c, half * slab:], fwd_s.at[c, 1])
        wait(gsx.at[c, cap:], grp_s.at[c, 0])
        wait(gsy.at[c, cap:], grp_s.at[c, 1])
    for i in range(2 * ITERS):
        wait(st_send.at[i], st_s.at[i])


def body(rows, top_ids, border_ids, centroids, mass):
    M = lax.axis_size("member")
    G = lax.axis_size("group")
    tok, D = rows.shape
    C, SUB = mass.shape
    cap = 2 * tok // G
    slots = G * cap
    W = D // CHUNKS
    span = max(LANES, cap)
    vmem = pl.BlockSpec(memory_space=pltpu.VMEM)
    dma = pltpu.SemaphoreType.DMA
    pool = pltpu.VMEM((CHUNKS, 2 * tok, W // 2), BF16)
    grouped = pltpu.VMEM((CHUNKS, slots, W), BF16)
    codes = pltpu.VMEM((M, 1, LANES), I32)
    locals_ = pltpu.VMEM((G, 1, span), I32)
    lane = pltpu.VMEM((1, slots), I32)
    stats = pltpu.VMEM((2 * ITERS, 1, 2 * slots), F32)
    refined, new_mass = pl.pallas_call(
        functools.partial(kernel, M, G),
        out_shape=(jax.ShapeDtypeStruct((C * SUB, D), F32), jax.ShapeDtypeStruct((C, SUB), F32)),
        in_specs=[vmem] * 5,
        out_specs=(vmem, vmem),
        scratch_shapes=[
            pool, pool, pool, grouped, grouped, grouped, grouped,
            codes, codes, codes, locals_, locals_, lane, lane, stats, stats,
            dma((2,)), dma((2,)), dma((2,)), dma((2,)),
            dma((CHUNKS, 2)), dma((CHUNKS, 2)), dma((CHUNKS, 2)), dma((CHUNKS, 2)),
            dma, dma, dma((CHUNKS, 2)), dma((CHUNKS, 2)), dma, dma,
            dma((2 * ITERS,)), dma((2 * ITERS,)),
        ],
        compiler_params=pltpu.CompilerParams(
            collective_id=0, has_side_effects=True, vmem_limit_bytes=48 * 1024 * 1024),
    )(rows, top_ids.reshape(1, tok), border_ids.reshape(1, C),
      centroids.reshape(C * SUB, D), mass)
    return refined.reshape(C, SUB, D), new_mass


def solution(mesh):
    in_specs = (
        P(("group", "member"), None),
        P(("group", "member")),
        P(("group", "member")),
        P(("group", "member"), None, None),
        P(("group", "member"), None),
    )
    out_specs = (P(("group", "member"), None, None), P(("group", "member"), None))
    return jax.shard_map(body, mesh=mesh, in_specs=in_specs, out_specs=out_specs, check_vma=False)
```

time: 248 us -> 125 us (0.50)
  the two profiles are of different devices: /device:TPU:32 before, /device:TPU:24 now
where the time goes in v1:
time: 125 us
  Pallas kernels  120 us (96%)
  local copies, waits for them, and re-layouts  4.31 us (3%)
    pallas_call x1, Pallas kernels, body(): pl.pallas_call(functools.partial(kernel, M, G), out_shape=(jax.ShapeDtype...  120 us
    unnamed x12, local copies, waits for them, and re-layouts  4.31 us

profile of v1, /device:TPU:24, one launch (start us, length us, event | category | flops | bytes accessed | tf_op | source)
XLA Modules:
  0.0 125.1 jit_solution(4495261672131328327)
XLA Ops:
  0.6 0.0 copy-start.2
  0.6 0.0 copy-start.3
  0.7 0.0 copy-start.4
  0.7 0.7 copy-done.2
  1.3 0.0 copy-done.3
  1.3 0.0 copy-done.4
  1.3 0.0 copy-start
  1.3 1.0 copy-done
  2.4 0.0 copy-start.1
  2.4 1.0 copy-done.1
  3.4 120.1 %shard_map.68 = (f32[256,1024]{1,0:T(8,128)S(1)}, f32[4,64]{1,0:T(4,128)S(1)}) custom-call(bf16[256,1024]{1,0:T(8,128)(2,1)S(1)} %copy-done, s32[1,256]{1,0:T(1,128)S(1)} %bitcast.6, s32[1,4]{1,0:T(1,128)S(1)} %bitcast.7, bf16[256,1024]{1,0:T(8,128)(2,1)S(1)} %bitcast.5, f32[4,64]{1,0:T(4,128)S(1)} %copy-done.2), custom_call_target="tpu_custom_call" | custom-call | tf_op jit(solution)/shard_map/pallas_call | solution.py:335
  123.5 1.0 copy.9
  124.5 0.6 copy.10
Async XLA Ops:
  0.6 0.7 copy-start.2
  0.6 0.7 copy-start.3
  0.7 0.7 copy-start.4
  1.3 1.0 copy-start
  2.4 1.0 copy-start.1

commit v2 on v1

--- a/solution.py
+++ b/solution.py
@@ -13,7 +13,8 @@
 BALANCE = 1.0
 KEEP = 0.5
 
-CHUNKS = 2
+CHUNKS = 4
+NEAR = 7
 LANES = 128
 LOW = -1e30
 MESH = pl.DeviceIdType.MESH
@@ -55,27 +56,28 @@
 
 def kernel(
     M, G,
-    rows_ref, ids_ref, border_ref, cent_ref, mass_ref,
+    rows_hbm, ids_ref, border_ref, cent_hbm, mass_ref,
     out_ref, mass_out_ref,
-    rsend, ra, rb, gsx, gsy, x, y,
+    rows_ref, cent_ref, rsend, ra, rb, gsx, gsy, x, y,
     idmsg, ida, idb, locmsg, locx, ymsg, yrecv, st_send, st_recv,
     ids_s, ids_r, idf_s, idf_r, row_s, row_r, fwd_s, fwd_r,
-    loc_s, loc_r, grp_s, grp_r, y_s, y_r, st_s, st_r,
+    loc_s, loc_r, grp_s, grp_r, y_s, y_r, st_s, st_r, in_sem,
 ):
-    tok, D = rows_ref.shape
+    tok, D = rows_hbm.shape
     C, SUB = mass_ref.shape
     K = C * SUB
     pm = tok // M
     slab = 2 * pm
     half = M // 2
+    near = min(NEAR, half - 1)
     cap = 2 * tok // G
     slots = G * cap
     W = D // CHUNKS
     H = W // 2
     g = lax.axis_index("group")
     m = lax.axis_index("member")
-    right = {"member": (m + 1) % M}
-    left = {"member": (m + M - 1) % M}
+    right = {"member": (m + 1) & (M - 1)}
+    left = {"member": (m + M - 1) & (M - 1)}
 
     def remote(src, dst, ssem, rsem, dev):
         return pltpu.make_async_remote_copy(
@@ -89,11 +91,16 @@
 
     @pl.loop(1, M)
     def _(d):
-        pl.semaphore_signal(barrier, inc=1, device_id={"member": (m + d) % M}, device_id_type=MESH)
+        pl.semaphore_signal(barrier, inc=1, device_id={"member": (m + d) & (M - 1)}, device_id_type=MESH)
 
     @pl.loop(1, G)
     def _(j):
-        pl.semaphore_signal(barrier, inc=1, device_id={"group": (g + j) % G}, device_id_type=MESH)
+        pl.semaphore_signal(barrier, inc=1, device_id={"group": (g + j) & (G - 1)}, device_id_type=MESH)
+
+    rows_in = pltpu.make_async_copy(rows_hbm, rows_ref, in_sem.at[0])
+    cent_in = pltpu.make_async_copy(cent_hbm, cent_ref, in_sem.at[1])
+    rows_in.start()
+    cent_in.start()
 
     ids = ids_ref[...]
     rel = (((ids >> log2(C)) & (M - 1)) - m) & (M - 1)
@@ -115,14 +122,15 @@
         rsend[c] = (dot(pick0, rows_ref[:, c * W:c * W + H])
                     + dot(pick1, rows_ref[:, c * W + H:(c + 1) * W])).astype(BF16)
 
+    rows_in.wait()
     order_rows(0)
     pl.semaphore_wait(barrier, M - 1 + G - 1)
 
     @pl.loop(1, half)
     def _(d):
-        remote(idmsg.at[d], ida.at[d], ids_s.at[0], ids_r.at[0], {"member": (m + d) % M}).start()
+        remote(idmsg.at[d], ida.at[d], ids_s.at[0], ids_r.at[0], {"member": (m + d) & (M - 1)}).start()
         e = M - 1 - d
-        remote(idmsg.at[e], idb.at[e], ids_s.at[1], ids_r.at[1], {"member": (m + M - d) % M}).start()
+        remote(idmsg.at[e], idb.at[e], ids_s.at[1], ids_r.at[1], {"member": (m + M - d) & (M - 1)}).start()
 
     ida[0] = idmsg[0]
     idb[M - 1] = idmsg[M - 1]
@@ -131,20 +139,21 @@
         return pl.ds(pl.multiple_of(d * slab, slab), slab)
 
     def send_rows(c):
-        @pl.loop(1, half)
-        def _(d):
-            e = M - 1 - d
-            remote(rsend.at[c, at(d)], ra.at[c, at(d)], row_s.at[c, 0], row_r.at[c, 0],
-                   {"member": (m + d) % M}).start()
-            remote(rsend.at[c, at(e)], rb.at[c, at(e)], row_s.at[c, 1], row_r.at[c, 1],
-                   {"member": (m + M - d) % M}).start()
+        for first, last, which in ((1, near, 0), (near, half, 1)):
+            @pl.loop(first, last)
+            def _(d):
+                e = M - 1 - d
+                remote(rsend.at[c, at(d)], ra.at[c, at(d)], row_s.at[c, 0], row_r.at[c, which],
+                       {"member": (m + d) & (M - 1)}).start()
+                remote(rsend.at[c, at(e)], rb.at[c, at(e)], row_s.at[c, 1], row_r.at[c, 2 + which],
+                       {"member": (m + M - d) & (M - 1)}).start()
+
         ra[c, 0:slab] = rsend[c, 0:slab]
         rb[c, (M - 1) * slab:] = rsend[c, (M - 1) * slab:]
 
     send_rows(0)
     for c in range(1, CHUNKS):
         order_rows(c)
-        send_rows(c)
 
     wait(ida.at[1:half], ids_r.at[0])
     remote(ida.at[0:half], idb.at[0:half], idf_s.at[0], idf_r.at[0], right).start()
@@ -152,6 +161,8 @@
     remote(idb.at[half:M], ida.at[half:M], idf_s.at[1], idf_r.at[1], left).start()
     wait(ida.at[half:M], idf_r.at[1])
     wait(idb.at[0:half], idf_r.at[0])
+    if CHUNKS > 1:
+        send_rows(1)
 
     def group_place(ref):
         code = jnp.concatenate(
@@ -179,31 +190,37 @@
 
     @pl.loop(1, G)
     def _(j):
-        remote(locmsg.at[j], locx.at[j], loc_s, loc_r, {"group": (g + j) % G}).start()
+        remote(locmsg.at[j], locx.at[j], loc_s, loc_r, {"group": (g + j) & (G - 1)}).start()
 
     locx[0] = locmsg[0]
     xp = group_picks(toward, rank)
     _, toward_b, rank_b = group_place(idb)
     yp = group_picks(toward_b, rank_b)
 
-    wait(locx.at[1:G], loc_r)
-    local = jnp.concatenate(
-        [jnp.sum(locx[b * pj:(b + 1) * pj], axis=0) for b in range(slots // span)], axis=1) - 1
-    base = (g * M + m) * C
-    edge = jnp.full((1, slots), -1, I32)
-    for k in range(C):
-        edge = jnp.where(local == k, border_ref[:, k:k + 1] - base, edge)
-    ymsg[...] = jnp.where(local >= 0, edge - C, -1)
-    remote(ymsg, yrecv, y_s, y_r, right).start()
+    def share_local():
+        wait(locx.at[1:G], loc_r)
+        local = jnp.concatenate(
+            [jnp.sum(locx[b * pj:(b + 1) * pj], axis=0) for b in range(slots // span)], axis=1) - 1
+        base = (g * M + m) * C
+        edge = jnp.full((1, slots), -1, I32)
+        for k in range(C):
+            edge = jnp.where(local == k, border_ref[:, k:k + 1] - base, edge)
+        ymsg[...] = jnp.where(local >= 0, edge - C, -1)
+        remote(ymsg, yrecv, y_s, y_r, right).start()
+        return local, edge
 
     def gat(j):
         return pl.ds(pl.multiple_of(j * cap, cap), cap)
 
+    def wait_near(c):
+        wait(ra.at[c, slab:near * slab], row_r.at[c, 0])
+        wait(rb.at[c, (M - near) * slab:(M - 1) * slab], row_r.at[c, 2])
+
     def forward(c):
-        wait(ra.at[c, slab:half * slab], row_r.at[c, 0])
+        wait(ra.at[c, near * slab:half * slab], row_r.at[c, 1])
         remote(ra.at[c, 0:half * slab], rb.at[c, 0:half * slab],
                fwd_s.at[c, 0], fwd_r.at[c, 0], right).start()
-        wait(rb.at[c, half * slab:(M - 1) * slab], row_r.at[c, 1])
+        wait(rb.at[c, half * slab:(M - near) * slab], row_r.at[c, 3])
         remote(rb.at[c, half * slab:], ra.at[c, half * slab:],
                fwd_s.at[c, 1], fwd_r.at[c, 1], left).start()
 
@@ -220,13 +237,20 @@
         @pl.loop(1, G)
         def _(j):
             remote(send.at[c, gat(j)], land.at[c, gat(j)], grp_s.at[c, which], grp_r.at[c, which],
-                   {"group": (g + j) % G}).start()
+                   {"group": (g + j) & (G - 1)}).start()
         land[c, 0:cap] = send[c, 0:cap]
 
+    wait_near(0)
     for c in range(CHUNKS):
         forward(c)
+        if c + 1 < CHUNKS:
+            wait_near(c + 1)
+        if c + 2 < CHUNKS:
+            send_rows(c + 2)
         regroup(c, 0)
         regroup(c, 1)
+        if c == 0:
+            local, edge = share_local()
 
     eye = iota((SUB, SUB), 0) == iota((SUB, SUB), 1)
 
@@ -240,6 +264,7 @@
     mask_x = (block == local) | (block == edge)
     mask_y = block == yrecv[...]
     mass_now = to_column(mass_ref[...])
+    cent_in.wait()
     for step in range(ITERS):
         bias = (BALANCE * jnp.log(mass_now)).astype(BF16).astype(F32)
         if step == 0:
@@ -325,6 +350,7 @@
     W = D // CHUNKS
     span = max(LANES, cap)
     vmem = pl.BlockSpec(memory_space=pltpu.VMEM)
+    anywhere = pl.BlockSpec(memory_space=pl.ANY)
     dma = pltpu.SemaphoreType.DMA
     pool = pltpu.VMEM((CHUNKS, 2 * tok, W // 2), BF16)
     grouped = pltpu.VMEM((CHUNKS, slots, W), BF16)
@@ -335,18 +361,18 @@
     refined, new_mass = pl.pallas_call(
         functools.partial(kernel, M, G),
         out_shape=(jax.ShapeDtypeStruct((C * SUB, D), F32), jax.ShapeDtypeStruct((C, SUB), F32)),
-        in_specs=[vmem] * 5,
+        in_specs=[anywhere, vmem, vmem, anywhere, vmem],
         out_specs=(vmem, vmem),
         scratch_shapes=[
-            pool, pool, pool, grouped, grouped, grouped, grouped,
+            pltpu.VMEM((tok, D), BF16), pltpu.VMEM((C * SUB, D), BF16), pool, pool, pool, grouped, grouped, grouped, grouped,
             codes, codes, codes, locals_, locals_, lane, lane, stats, stats,
             dma((2,)), dma((2,)), dma((2,)), dma((2,)),
-            dma((CHUNKS, 2)), dma((CHUNKS, 2)), dma((CHUNKS, 2)), dma((CHUNKS, 2)),
+            dma((CHUNKS, 2)), dma((CHUNKS, 4)), dma((CHUNKS, 2)), dma((CHUNKS, 2)),
             dma, dma, dma((CHUNKS, 2)), dma((CHUNKS, 2)), dma, dma,
-            dma((2 * ITERS,)), dma((2 * ITERS,)),
+            dma((2 * ITERS,)), dma((2 * ITERS,)), dma((2,)),
         ],
         compiler_params=pltpu.CompilerParams(
-            collective_id=0, has_side_effects=True, vmem_limit_bytes=48 * 1024 * 1024),
+            collective_id=0, has_side_effects=True, vmem_limit_bytes=56 * 1024 * 1024),
     )(rows, top_ids.reshape(1, tok), border_ids.reshape(1, C),
       centroids.reshape(C * SUB, D), mass)
     return refined.reshape(C, SUB, D), new_mass

time: 125 us -> 114 us (0.912)
  the two profiles are of different devices: /device:TPU:24 before, /device:TPU:32 now
where the time goes in v2:
time: 114 us
  Pallas kernels  110 us (96%)
  local copies, waits for them, and re-layouts  2.89 us (3%)
    pallas_call x1, Pallas kernels, body(): pl.pallas_call(functools.partial(kernel, M, G), out_shape=(jax.ShapeDtype...  110 us
    unnamed x4, local copies, waits for them, and re-layouts  2.89 us

profile of v2, /device:TPU:32, one launch (start us, length us, event | category | flops | bytes accessed | tf_op | source)
XLA Modules:
  0.0 113.7 jit_solution(9294109079929338682)
XLA Ops:
  0.6 110.2 %shard_map.68 = (f32[256,1024]{1,0:T(8,128)}, f32[4,64]{1,0:T(4,128)}) custom-call(bf16[256,1024]{1,0:T(8,128)(2,1)} %rows_hbm.1, s32[1,256]{1,0:T(1,128)} %bitcast.6, s32[1,4]{1,0:T(1,128)} %bitcast.7, bf16[256,1024]{1,0:T(8,128)(2,1)} %bitcast.5, f32[4,64]{1,0:T(4,128)} %mass_ref.1), custom_call_target="tpu_custom_call" | custom-call | tf_op jit(solution)/shard_map/pallas_call | solution.py:361
  110.8 0.0 copy-start
  110.8 2.3 %copy.9 = f32[4,64,1024]{2,1,0:T(8,128)} copy(f32[4,64,1024]{2,1,0:T(8,128)} %bitcast.4) | data formatting | bytes 2097152
  113.1 0.0 copy-done
  113.1 0.6 copy.10
Async XLA Ops:
  110.8 2.3 %copy-start = (f32[4,64]{1,0:T(4,128)S(1)}, f32[4,64]{1,0:T(4,128)}, u32[]{:S(2)}) copy-start(f32[4,64]{1,0:T(4,128)} %get-tuple-element.9) | copy-start | bytes 3076

commit v3 on v2

--- a/solution.py
+++ b/solution.py
@@ -87,20 +87,20 @@
     def wait(ref, sem):
         pltpu.make_async_copy(ref, ref, sem).wait()
 
-    barrier = pltpu.get_barrier_semaphore()
-
-    @pl.loop(1, M)
-    def _(d):
-        pl.semaphore_signal(barrier, inc=1, device_id={"member": (m + d) & (M - 1)}, device_id_type=MESH)
-
-    @pl.loop(1, G)
-    def _(j):
-        pl.semaphore_signal(barrier, inc=1, device_id={"group": (g + j) & (G - 1)}, device_id_type=MESH)
-
     rows_in = pltpu.make_async_copy(rows_hbm, rows_ref, in_sem.at[0])
     cent_in = pltpu.make_async_copy(cent_hbm, cent_ref, in_sem.at[1])
     rows_in.start()
     cent_in.start()
+
+    barrier = pltpu.get_barrier_semaphore()
+
+    @pl.loop(1, M)
+    def _(d):
+        pl.semaphore_signal(barrier, inc=1, device_id={"member": (m + d) & (M - 1)}, device_id_type=MESH)
+
+    @pl.loop(1, G)
+    def _(j):
+        pl.semaphore_signal(barrier, inc=1, device_id={"group": (g + j) & (G - 1)}, device_id_type=MESH)
 
     ids = ids_ref[...]
     rel = (((ids >> log2(C)) & (M - 1)) - m) & (M - 1)
@@ -154,6 +154,8 @@
     send_rows(0)
     for c in range(1, CHUNKS):
         order_rows(c)
+        if c == 1:
+            send_rows(c)
 
     wait(ida.at[1:half], ids_r.at[0])
     remote(ida.at[0:half], idb.at[0:half], idf_s.at[0], idf_r.at[0], right).start()
@@ -161,8 +163,6 @@
     remote(idb.at[half:M], ida.at[half:M], idf_s.at[1], idf_r.at[1], left).start()
     wait(ida.at[half:M], idf_r.at[1])
     wait(idb.at[0:half], idf_r.at[0])
-    if CHUNKS > 1:
-        send_rows(1)
 
     def group_place(ref):
         code = jnp.concatenate(
@@ -214,14 +214,18 @@
 
     def wait_near(c):
         wait(ra.at[c, slab:near * slab], row_r.at[c, 0])
+        remote(ra.at[c, 0:near * slab], rb.at[c, 0:near * slab],
+               fwd_s.at[c, 0], fwd_r.at[c, 0], right).start()
         wait(rb.at[c, (M - near) * slab:(M - 1) * slab], row_r.at[c, 2])
+        remote(rb.at[c, (M - near) * slab:], ra.at[c, (M - near) * slab:],
+               fwd_s.at[c, 1], fwd_r.at[c, 1], left).start()
 
     def forward(c):
         wait(ra.at[c, near * slab:half * slab], row_r.at[c, 1])
-        remote(ra.at[c, 0:half * slab], rb.at[c, 0:half * slab],
+        remote(ra.at[c, near * slab:half * slab], rb.at[c, near * slab:half * slab],
                fwd_s.at[c, 0], fwd_r.at[c, 0], right).start()
         wait(rb.at[c, half * slab:(M - near) * slab], row_r.at[c, 3])
-        remote(rb.at[c, half * slab:], ra.at[c, half * slab:],
+        remote(rb.at[c, half * slab:(M - near) * slab], ra.at[c, half * slab:(M - near) * slab],
                fwd_s.at[c, 1], fwd_r.at[c, 1], left).start()
 
     def regroup(c, which):
@@ -274,6 +278,7 @@
             scoring = out_ref[...].astype(BF16)
             state = out_ref[...]
         norm = jnp.sum(jnp.square(scoring[...].astype(F32)), axis=1, keepdims=True)
+        shift = norm * (1.0 / SOFTMAX_HEAT) + bias
         lx = jnp.zeros((K, slots), F32)
         ly = jnp.zeros((K, slots), F32)
         for c in range(CHUNKS):
@@ -286,7 +291,7 @@
             ly = ly + dot_t(part, y[c])
 
         def local_terms(product, mask, slot_at):
-            logit = jnp.where(mask, (2.0 * product - norm) / SOFTMAX_HEAT - bias, LOW)
+            logit = jnp.where(mask, product * (2.0 / SOFTMAX_HEAT) - shift, LOW)
             top = jnp.max(logit, axis=0, keepdims=True)
             expo = jnp.where(mask, jnp.exp(logit - top), 0.0)
             total = jnp.sum(expo, axis=0, keepdims=True)

time: 114 us -> 110 us (0.965)
  Pallas kernels: 110 us -> 107 us
    pallas_call x1, Pallas kernels: 110 us -> 107 us  [body(): pl.pallas_call(functools.partial(kernel, M, G), out_shape=(jax.ShapeDtype...]
where the time goes in v3:
time: 110 us
  Pallas kernels  107 us (97%)
  local copies, waits for them, and re-layouts  2.89 us (3%)
    pallas_call x1, Pallas kernels, body(): pl.pallas_call(functools.partial(kernel, M, G), out_shape=(jax.ShapeDtype...  107 us
    unnamed x4, local copies, waits for them, and re-layouts  2.89 us

profile of v3, /device:TPU:32, one launch (start us, length us, event | category | flops | bytes accessed | tf_op | source)
XLA Modules:
  0.0 110.3 jit_solution(15702368589633339752)
XLA Ops:
  0.6 106.7 %shard_map.68 = (f32[256,1024]{1,0:T(8,128)}, f32[4,64]{1,0:T(4,128)}) custom-call(bf16[256,1024]{1,0:T(8,128)(2,1)} %rows_hbm.1, s32[1,256]{1,0:T(1,128)} %bitcast.6, s32[1,4]{1,0:T(1,128)} %bitcast.7, bf16[256,1024]{1,0:T(8,128)(2,1)} %bitcast.5, f32[4,64]{1,0:T(4,128)} %mass_ref.1), custom_call_target="tpu_custom_call" | custom-call | tf_op jit(solution)/shard_map/pallas_call | solution.py:366
  107.4 0.0 copy-start
  107.4 2.3 %copy.9 = f32[4,64,1024]{2,1,0:T(8,128)} copy(f32[4,64,1024]{2,1,0:T(8,128)} %bitcast.4) | data formatting | bytes 2097152
  109.7 0.0 copy-done
  109.7 0.6 copy.10
Async XLA Ops:
  107.4 2.3 %copy-start = (f32[4,64]{1,0:T(4,128)S(1)}, f32[4,64]{1,0:T(4,128)}, u32[]{:S(2)}) copy-start(f32[4,64]{1,0:T(4,128)} %get-tuple-element.9) | copy-start | bytes 3076
